TPU v7x, 32 devices: a whole 2x2x4 slice. The times are simulated.
32 devices in a mesh: dp: 8 (over z, x), tensor: 4 (over y, core).
Axes of the slice: x: 2, y: 2, z: 4, core: 2. Of those that a mesh axis runs over, the one named last changes fastest.
Arguments:
- tokens_in: bfloat16 [12288, 768], P('dp'), may hold values from -6 to 6
- cotangent: bfloat16 [12288, 768], P('dp'), may hold values from -6 to 6
- span_mask: int32 [12288], P('dp'), may hold values from 0 to 1, as said below
- lengths: int32 [24], P('dp'), may hold values from 128 to 512, as said below
- step: int32 [1], replicated, may hold values from 1000 to 31999
- warmup: int32 [1], replicated, may hold values from 1000 to 29999
- total: int32 [1], replicated, may hold values from 32000 to 40000
- w_qkv: float32 [768, 3, 768], P(None, None, 'tensor'), may hold values from -0.21875 to 0.21875
- w_out: float32 [768, 768], P(None, 'tensor'), may hold values from -1.25 to 1.25
- w_in: float32 [768, 3072], P(None, 'tensor'), may hold values from -0.21875 to 0.21875
- w_back: float32 [768, 3072], P(None, 'tensor'), may hold values from -0.109375 to 0.109375
- gains: float32 [2, 768], replicated, may hold values from 0.5 to 1.5
- biases: float32 [6, 768], replicated, may hold values from -3 to 3
- bias_in: float32 [3072], replicated, may hold values from -3 to 3
- mom_qkv: float32 [2, 768, 3, 768], P(None, 'dp', None, 'tensor'), as said below
- mom_out: float32 [2, 768, 768], P(None, 'dp', 'tensor'), as said below
- mom_in: float32 [2, 768, 3072], P(None, 'dp', 'tensor'), as said below
- mom_back: float32 [2, 768, 3072], P(None, 'dp', 'tensor'), as said below
- mom_gains: float32 [2, 2, 768], replicated, as said below
- mom_biases: float32 [2, 6, 768], replicated, as said below
- mom_bias_in: float32 [2, 3072], replicated, as said below
Outputs:
- normed_out: bfloat16 [12288, 768], P('dp')
- input_grad: float32 [12288, 768], P('dp')
- change_qkv: float32 [768, 3, 768], P(None, None, 'tensor')
- change_out_proj: float32 [768, 768], P(None, 'tensor')
- change_in_proj: float32 [768, 3072], P(None, 'tensor')
- change_back_proj: float32 [768, 3072], P(None, 'tensor')
- change_gains: float32 [2, 768], replicated
- change_biases: float32 [6, 768], replicated
- change_bias_in: float32 [3072], replicated
- new_mom_qkv: float32 [2, 768, 3, 768], P(None, 'dp', None, 'tensor')
- new_mom_out: float32 [2, 768, 768], P(None, 'dp', 'tensor')
- new_mom_in: float32 [2, 768, 3072], P(None, 'dp', 'tensor')
- new_mom_back: float32 [2, 768, 3072], P(None, 'dp', 'tensor')
- new_mom_gains: float32 [2, 2, 768], replicated
- new_mom_biases: float32 [2, 6, 768], replicated
- new_mom_bias_in: float32 [2, 3072], replicated
Inputs may be any that keep to these rules, and one draw needn't show every extreme that they name: `span_mask`: marked positions lie below their sequence's length and form unions of spans of 1 to 10 positions; each sequence has at most 76 of them, and in every draw each of the 3 sequences of some index of dp has exactly 76. `lengths`: a sequence's real tokens stand at its start, the rest is padding. step < total. warmup < total. `mom_qkv`: index 1 of the leading dimension holds positive second moments. `mom_out`: index 1 of the leading dimension holds positive second moments. `mom_in`: index 1 of the leading dimension holds positive second moments. `mom_back`: index 1 of the leading dimension holds positive second moments. `mom_gains`: index 1 of the leading dimension holds positive second moments. `mom_biases`: index 1 of the leading dimension holds positive second moments. `mom_bias_in`: index 1 of the leading dimension holds positive second moments.
All inputs are finite; a program needn't handle non-finite values.
Results may differ from a plain program's by a relative error of at most 0.017.
The roundings to bfloat16 on the way count: a program that leaves them out, or rounds other values in their place, can miss the bound.
Values sent between devices are 32-bit elements; how exact they have to be, the bound alone decides.
A program may use at most 128 MiB of HBM per device.

v0:
```python
import math
import jax
import jax.numpy as jnp
from jax import lax
from jax.sharding import PartitionSpec as P

HD = 64
NORM_EPS = 1e-12
BETA_ONE = 0.9
BETA_TWO = 0.999
ADAM_EPS = 1e-06
WEIGHT_DECAY = 0.01


def layer_norm(values, gain, shift):
    center = values - jnp.mean(values, axis=-1, keepdims=True)
    spread = jnp.mean(center * center, axis=-1, keepdims=True)
    return center * lax.rsqrt(spread + NORM_EPS) * gain + shift


def exact_gelu(values):
    return jax.nn.gelu(values, approximate=False)


def outer_sum(left, right):
    return jnp.einsum("ta,tb->ab", left, right, preferred_element_type=jnp.float32)


def adam_step(weight, grad, moments, ratio, corr_one, corr_two, decay):
    first = BETA_ONE * moments[0] + (1.0 - BETA_ONE) * grad
    second = BETA_TWO * moments[1] + (1.0 - BETA_TWO) * grad * grad
    update = first / corr_one / (jnp.sqrt(second / corr_two) + ADAM_EPS) + decay * weight
    return (-ratio * update, jnp.stack([first, second]))


def on_device(
    tokens_in,
    cotangent,
    span_mask,
    lengths,
    step,
    warmup,
    total,
    w_qkv,
    w_out,
    w_in,
    w_back,
    gains,
    biases,
    bias_in,
    mom_qkv,
    mom_out,
    mom_in,
    mom_back,
    mom_gains,
    mom_biases,
    mom_bias_in,
):
    row_count, model_width = tokens_in.shape
    seq_count = lengths.shape[0]
    seq_length = row_count // seq_count
    head_cols = w_qkv.shape[2]
    hidden_cols = w_in.shape[1]
    head_size = HD
    local_heads = head_cols // head_size
    query_scale = 1.0 / math.sqrt(head_size)
    tensor_slot = lax.axis_index("tensor")
    bias_query = lax.dynamic_slice_in_dim(biases[0], tensor_slot * head_cols, head_cols)
    bias_value = lax.dynamic_slice_in_dim(biases[1], tensor_slot * head_cols, head_cols)
    bias_hidden = lax.dynamic_slice_in_dim(bias_in, tensor_slot * hidden_cols, hidden_cols)
    qkv_low = w_qkv.astype(jnp.bfloat16).reshape(model_width, 3 * head_cols)
    out_low = w_out.astype(jnp.bfloat16)
    in_low = w_in.astype(jnp.bfloat16)
    down_low = w_back.astype(jnp.bfloat16)
    projected = jnp.dot(tokens_in, qkv_low, preferred_element_type=jnp.float32).reshape(
        row_count, 3, head_cols
    )
    attn_shape = (seq_count, seq_length, local_heads, head_size)
    queries = (
        ((projected[:, 0] + bias_query) * query_scale).astype(jnp.bfloat16).reshape(attn_shape)
    )
    keys = projected[:, 1].astype(jnp.bfloat16).reshape(attn_shape)
    values = (projected[:, 2] + bias_value).astype(jnp.bfloat16).reshape(attn_shape)
    positions = jnp.arange(seq_length, dtype=jnp.int32)
    inside = positions[None, :] < lengths[:, None]
    key_bias = jnp.where(inside, 0.0, -1000000000.0).astype(jnp.float32)

    def score_block():
        raw = jnp.einsum("sqhd,skhd->shqk", queries, keys, preferred_element_type=jnp.float32)
        return raw + key_bias[:, None, None, :]

    scores = score_block()
    peak = jnp.max(scores, axis=-1, keepdims=True)
    log_total = peak + jnp.log(jnp.sum(jnp.exp(scores - peak), axis=-1, keepdims=True))
    probs_low = jnp.exp(scores - log_total).astype(jnp.bfloat16)
    context_low = (
        jnp.einsum("shqk,skhd->sqhd", probs_low, values, preferred_element_type=jnp.float32)
        .reshape(row_count, head_cols)
        .astype(jnp.bfloat16)
    )
    attn_part = jnp.einsum("tc,dc->td", context_low, out_low, preferred_element_type=jnp.float32)
    attn_sum = lax.psum(attn_part, "tensor")
    residual_one = tokens_in.astype(jnp.float32) + attn_sum + biases[2]
    normed = layer_norm(residual_one, gains[0], biases[3])
    normed_low = normed.astype(jnp.bfloat16)
    pre_act = jnp.dot(normed_low, in_low, preferred_element_type=jnp.float32) + bias_hidden
    act_low = exact_gelu(pre_act).astype(jnp.bfloat16)
    down_part = jnp.einsum("tf,df->td", act_low, down_low, preferred_element_type=jnp.float32)
    down_sum = lax.psum(down_part, "tensor")
    residual_two = normed + down_sum + biases[4]
    result, norm_two_back = jax.vjp(layer_norm, residual_two, gains[1], biases[5])
    normed_out = result.astype(jnp.bfloat16)
    live_int = inside.reshape(row_count).astype(jnp.int32) * span_mask
    live = live_int.astype(jnp.float32)
    grad_result = cotangent.astype(jnp.float32) * live[:, None]
    d_res_two, d_gain_two, d_shift_two = norm_two_back(grad_result)
    d_res_two_low = d_res_two.astype(jnp.bfloat16)
    grad_back = outer_sum(d_res_two_low, act_low)
    d_act = jnp.dot(d_res_two_low, down_low, preferred_element_type=jnp.float32)
    _, gelu_back = jax.vjp(exact_gelu, pre_act)
    d_pre = gelu_back(d_act)[0]
    d_pre_low = d_pre.astype(jnp.bfloat16)
    grad_in = outer_sum(normed_low, d_pre_low)
    d_normed_part = jnp.einsum("tf,df->td", d_pre_low, in_low, preferred_element_type=jnp.float32)
    d_normed = lax.psum(d_normed_part, "tensor") + d_res_two
    _, norm_one_back = jax.vjp(layer_norm, residual_one, gains[0], biases[3])
    d_res_one, d_gain_one, d_shift_one = norm_one_back(d_normed)
    d_res_one_low = d_res_one.astype(jnp.bfloat16)
    grad_out_proj = outer_sum(d_res_one_low, context_low)
    d_context = (
        jnp.dot(d_res_one_low, out_low, preferred_element_type=jnp.float32)
        .astype(jnp.bfloat16)
        .reshape(attn_shape)
    )
    probs = jnp.exp(score_block() - log_total)
    probs_again = probs.astype(jnp.bfloat16)
    d_probs = jnp.einsum("sqhd,skhd->shqk", d_context, values, preferred_element_type=jnp.float32)
    d_values = jnp.einsum(
        "shqk,sqhd->skhd", probs_again, d_context, preferred_element_type=jnp.float32
    ).reshape(row_count, head_cols)
    d_scores = (probs * (d_probs - jnp.sum(probs * d_probs, axis=-1, keepdims=True))).astype(
        jnp.bfloat16
    )
    d_queries = (
        jnp.einsum("shqk,skhd->sqhd", d_scores, keys, preferred_element_type=jnp.float32).reshape(
            row_count, head_cols
        )
        * query_scale
    )
    d_keys = jnp.einsum(
        "shqk,sqhd->skhd", d_scores, queries, preferred_element_type=jnp.float32
    ).reshape(row_count, head_cols)
    d_proj_low = (
        jnp.stack([d_queries, d_keys, d_values], axis=1)
        .astype(jnp.bfloat16)
        .reshape(row_count, 3 * head_cols)
    )
    grad_qkv = outer_sum(tokens_in, d_proj_low).reshape(model_width, 3, head_cols)
    d_entry_part = jnp.einsum("tc,dc->td", d_proj_low, qkv_low, preferred_element_type=jnp.float32)
    input_grad = lax.psum(d_entry_part, "tensor") + d_res_one
    first_rank = (tensor_slot == 0).astype(jnp.float32)
    width_zero = jnp.zeros((model_width,), jnp.float32)

    def place_heads(partial_sum):
        return lax.dynamic_update_slice_in_dim(width_zero, partial_sum, tensor_slot * head_cols, 0)

    grad_gains = jnp.stack([d_gain_one, d_gain_two]) * first_rank
    grad_biases = jnp.stack(
        [
            place_heads(jnp.sum(d_queries, axis=0)),
            place_heads(jnp.sum(d_values, axis=0)),
            jnp.sum(d_res_one, axis=0) * first_rank,
            d_shift_one * first_rank,
            jnp.sum(d_res_two, axis=0) * first_rank,
            d_shift_two * first_rank,
        ]
    )
    grad_bias_in = lax.dynamic_update_slice_in_dim(
        jnp.zeros(bias_in.shape, jnp.float32), jnp.sum(d_pre, axis=0), tensor_slot * hidden_cols, 0
    )
    grad_gains, grad_biases, grad_bias_in = lax.psum(
        (grad_gains, grad_biases, grad_bias_in), ("dp", "tensor")
    )
    data_slot = lax.axis_index("dp")
    shard_rows = model_width // lax.axis_size("dp")
    summed = lax.psum((grad_qkv, grad_out_proj, grad_in, grad_back), "dp")
    owned = tuple(
        (
            lax.dynamic_slice_in_dim(whole_sum, data_slot * shard_rows, shard_rows, 0)
            for whole_sum in summed
        )
    )
    clock = step[0].astype(jnp.float32)
    warm = warmup[0].astype(jnp.float32)
    horizon = total[0].astype(jnp.float32)
    ratio = jnp.minimum(clock / warm, (horizon - clock) / (horizon - warm))
    corr_one = 1.0 - jnp.power(BETA_ONE, clock)
    corr_two = 1.0 - jnp.power(BETA_TWO, clock)
    change_rows = []
    fresh_moments = []
    for weight, grad_rows, moment in zip(
        (w_qkv, w_out, w_in, w_back), owned, (mom_qkv, mom_out, mom_in, mom_back)
    ):
        weight_rows = lax.dynamic_slice_in_dim(weight, data_slot * shard_rows, shard_rows, 0)
        row_change, new_moment = adam_step(
            weight_rows, grad_rows, moment, ratio, corr_one, corr_two, WEIGHT_DECAY
        )
        change_rows.append(row_change)
        fresh_moments.append(new_moment)
    change_qkv, change_out_proj, change_in_proj, change_back_proj = (
        lax.all_gather(change_rows[0], "dp", axis=0, tiled=True),
        lax.all_gather(change_rows[1], "dp", axis=0, tiled=True),
        lax.all_gather(change_rows[2], "dp", axis=0, tiled=True),
        lax.all_gather(change_rows[3], "dp", axis=0, tiled=True),
    )
    change_gains, new_mom_gains = adam_step(
        gains, grad_gains, mom_gains, ratio, corr_one, corr_two, 0.0
    )
    change_biases, new_mom_biases = adam_step(
        biases, grad_biases, mom_biases, ratio, corr_one, corr_two, 0.0
    )
    change_bias_in, new_mom_bias_in = adam_step(
        bias_in, grad_bias_in, mom_bias_in, ratio, corr_one, corr_two, 0.0
    )
    return (
        normed_out,
        input_grad,
        change_qkv,
        change_out_proj,
        change_in_proj,
        change_back_proj,
        change_gains,
        change_biases,
        change_bias_in,
        fresh_moments[0],
        fresh_moments[1],
        fresh_moments[2],
        fresh_moments[3],
        new_mom_gains,
        new_mom_biases,
        new_mom_bias_in,
    )


def solution(mesh):
    in_specs = (
        P("dp", None),
        P("dp", None),
        P("dp"),
        P("dp"),
        P(),
        P(),
        P(),
        P(None, None, "tensor"),
        P(None, "tensor"),
        P(None, "tensor"),
        P(None, "tensor"),
        P(),
        P(),
        P(),
        P(None, "dp", None, "tensor"),
        P(None, "dp", "tensor"),
        P(None, "dp", "tensor"),
        P(None, "dp", "tensor"),
        P(),
        P(),
        P(),
    )
    out_specs = (
        P("dp", None),
        P("dp", None),
        P(None, None, "tensor"),
        P(None, "tensor"),
        P(None, "tensor"),
        P(None, "tensor"),
        P(),
        P(),
        P(),
        P(None, "dp", None, "tensor"),
        P(None, "dp", "tensor"),
        P(None, "dp", "tensor"),
        P(None, "dp", "tensor"),
        P(),
        P(),
        P(),
    )
    return jax.shard_map(
        on_device, mesh=mesh, in_specs=in_specs, out_specs=out_specs, check_vma=False
    )
```

profile of v0, /device:TPU:0, one launch (start us, length us, event | category | flops | bytes accessed | tf_op | source)
XLA Modules:
  0.0 939.9 jit_solution(9173336511828967916)
XLA Ops:
  7.2 3.8 fusion.10
  11.1 1.2 fusion.80
  12.6 1.1 convert_element_type.98
  13.8 0.9 squeeze.4
  14.7 1.9 squeeze.5
  16.6 2.9 add_reduce_fusion
  19.6 1.8 exponential_reduce_fusion
  21.8 1.4 copy-done
  23.2 1.7 fusion.12
  25.6 3.0 fusion.45
  28.9 0.8 dynamic_slice.35
  29.7 95.8 %all-reduce.8.cloned.1.call-done = f32[1536,768]{1,0:T(8,128)} async-done(((f32[1536,768]{1,0:T(8,128)}), f32[1536,768]{1,0:T(8,128)}) %all-reduce.8.cloned.1.call-update) | async-done | bytes 4718608 | tf_op jit(solution)/shard_map/psum | solution.py:102
  125.6 3.8 fusion.79
  129.4 0.7 multiply_reduce_fusion.6
  130.1 2.6 copy-done.19
  132.8 14.4 %multiply_convert_fusion.1 = (bf16[1536,768]{1,0:T(8,128)(2,1)S(1)}, f32[1536,768]{1,0:T(8,128)}, f32[1536,768]{1,0:T(8,128)}) fusion(f32[768]{0:T(1024)S(1)} %dynamic_slice.35, f32[768,768]{1,0:T(8,128)S(1)} %copy-done.19, f32[1536,768]{1,0:T(8,128)S(1)} %get-tuple-element.96, f32[768]{0:T(1024)S(1)} %get-tuple-element.125, ...), kind=kOutput, calls=%fused_computation.21 | convolution fusion | flops 1896284160 | bytes 18895872 | tf_op jit(solution)/shard_map/dot_general | solution.py:106
  147.1 1.4 copy-done.39
  148.5 4.3 fusion.24
  153.6 93.7 %all-reduce.10.cloned.1.call-done = f32[1536,768]{1,0:T(8,128)} async-done(((f32[1536,768]{1,0:T(8,128)}), f32[1536,768]{1,0:T(8,128)}) %all-reduce.10.cloned.1.call-update) | async-done | bytes 4718608 | tf_op jit(solution)/shard_map/psum | solution.py:109
  247.2 4.7 fusion.77
  252.6 1.0 copy-done.4
  253.6 2.8 multiply_reduce_fusion.1
  256.5 3.7 fusion.76
  260.2 4.5 fusion.85
  264.7 1.4 copy-done.40
  266.1 4.3 fusion.17
  270.5 6.9 fusion.72
  277.4 6.4 fusion.15
  283.8 81.0 %all-reduce.12.cloned.1.call-done = f32[1536,768]{1,0:T(8,128)} async-done(((f32[1536,768]{1,0:T(8,128)}), f32[1536,768]{1,0:T(8,128)}) %all-reduce.12.cloned.1.call-update) | async-done | bytes 4718608 | tf_op jit(solution)/shard_map/psum | solution.py:125
  364.8 7.5 multiply_reduce_fusion.2
  372.2 3.8 fusion.75
  376.1 2.4 fusion.73
  378.5 1.0 convolution_convert_fusion
  380.0 6.4 fusion.84
  386.4 5.7 multiply_reduce_fusion
  392.2 2.3 multiply_convert_fusion
  394.5 1.6 convolution_bitcast_fusion.2
  396.1 1.6 fusion.83
  398.2 0.8 stack_reshape.7
  399.5 1.0 mul.594
  401.0 0.8 stack_reshape.6
  402.1 4.4 fusion.88
  406.5 2.9 copy.94
  409.5 5.7 convolution_bitcast_fusion
  417.9 1.2 constant_dynamic-slice_fusion.1
  419.3 247.8 %all-reduce.16.cloned.1.call-done = (f32[768,3,192]{2,0,1:T(8,128)}, f32[768,192]{1,0:T(8,128)}, f32[768,768]{1,0:T(8,128)}, f32[768,768]{1,0:T(8,128)}) async-done(((f32[768,3,192]{2,0,1:T(8,128)}, f32[768,192]{1,0:T(8,128)}, f32[768,768]{1,0:T(8,128)}, f32[768,768]{1,0:T(8,128)}), (f32[768,3,192]{2,0,1:T(8,128)}, f32[768,192]{1,0:T(8,128)}, f32[768,768]{1,0:T(8,128)}, ...) | async-done | bytes 7077904 | tf_op jit(solution)/shard_map/psum | solution.py:186
  667.1 1.9 fusion.50
  669.1 2.0 fusion.48
  671.2 2.2 fusion.49
  674.7 87.7 %all-reduce.14.cloned.1.call-done = f32[1536,768]{1,0:T(8,128)} async-done(((f32[1536,768]{1,0:T(8,128)}), f32[1536,768]{1,0:T(8,128)}) %all-reduce.14.cloned.1.call-update) | async-done | bytes 4718608 | tf_op jit(solution)/shard_map/psum | solution.py:160
  762.4 6.5 add_reduce_fusion.1
  769.0 41.3 %all-reduce = (f32[2,768]{1,0:T(2,128)S(1)}, f32[6,768]{1,0:T(8,128)S(1)}, f32[3072]{0:T(1024)S(1)}) all-reduce(f32[2,768]{1,0:T(2,128)S(1)} %maximum_multiply_fusion, f32[6,768]{1,0:T(8,128)S(1)} %stack.89, f32[3072]{0:T(1024)S(1)} %dynamic_update_slice.13), channel_id=1, replica_groups=mesh['dp'=8,'tensor'=4] {'dp','tensor'}, use_global_device_ids=true, to_apply=%region_21.22 | all-reduce | flops 9216 | bytes 73728 | tf_op jit(solution)/shard_map/psum | solution.py:181
  814.1 1.0 fusion.58
  815.1 33.2 %all_gather.13 = f32[768,192]{1,0:T(8,128)S(1)} all-gather(f32[96,192]{1,0:T(8,128)S(1)} %get-tuple-element.114), channel_id=1, replica_groups=mesh['dp'=8,'tensor'=4] {'dp'}, dimensions={0}, use_global_device_ids=true | all-gather | bytes 663552 | tf_op jit(solution)/shard_map/all_gather | solution.py:212
  848.3 1.1 copy.100
  849.4 0.7 pad_maximum_fusion.3
  850.1 0.9 pad_maximum_fusion
  850.9 0.9 pad_maximum_fusion.2
  851.8 0.9 pad_maximum_fusion.1
  852.6 2.9 copy.99
  855.5 19.2 %all-gather.6.cloned.1.call-done = f32[768,768]{1,0:T(8,128)} async-done(((f32[96,768]{1,0:T(8,128)}), f32[768,768]{1,0:T(8,128)}) %all-gather.6.cloned.1.call-update) | async-done | bytes 2359312 | tf_op jit(solution)/shard_map/all_gather | solution.py:213
  874.7 53.4 %all-gather.8.cloned.1.call-done = f32[768,768]{1,0:T(8,128)} async-done(((f32[96,768]{1,0:T(8,128)}), f32[768,768]{1,0:T(8,128)}) %all-gather.8.cloned.1.call-update) | async-done | bytes 2359312 | tf_op jit(solution)/shard_map/all_gather | solution.py:214
  928.1 3.4 copy.176
  931.5 1.4 copy.177
  (173 shorter events, 10.9 us)
Async XLA Ops:
  7.2 118.4 %all-reduce.8.cloned.1.call-start = ((), (), s32[]{:S(2)}) async-start(), calls=%async_computation | async-start | bytes 9437184 | tf_op jit(solution)/shard_map/psum | solution.py:102
  11.0 1.3 copy-start.38
  11.0 1.3 copy-start.15
  12.6 6.9 copy-start.17
  19.6 3.6 copy-start
  21.4 3.5 copy-start.10
  23.2 1.8 copy-start.5
  23.2 2.4 copy-start.8
  28.7 1.0 copy-start.25
  28.7 218.5 %all-reduce.10.cloned.1.call-start = ((), (), s32[]{:S(2)}) async-start(), calls=%async_computation.1 | async-start | bytes 9437184 | tf_op jit(solution)/shard_map/psum | solution.py:109
  129.4 17.8 %copy-start.1 = (f32[1536,768]{1,0:T(8,128)}, f32[1536,768]{1,0:T(8,128)S(1)}, u32[]{:S(2)}) copy-start(f32[1536,768]{1,0:T(8,128)S(1)} %get-tuple-element.96) | copy-start | bytes 14155780
  129.4 3.4 copy-start.19
  132.8 15.8 %copy-start.21 = (f32[768,768]{1,0:T(8,128)S(1)}, f32[768,768]{1,0:T(8,128)}, u32[]{:S(2)}) copy-start(f32[768,768]{1,0:T(8,128)} %param.31) | copy-start | bytes 7077892
  147.1 1.4 copy-start.39
  152.9 0.7 copy-start.36
  152.9 211.9 %all-reduce.12.cloned.1.call-start = ((), (), s32[]{:S(2)}) async-start(), calls=%async_computation.2 | async-start | bytes 9437184 | tf_op jit(solution)/shard_map/psum | solution.py:125
  252.0 1.7 copy-start.4
  253.6 6.5 slice-start.3
  253.6 6.5 slice-start.5
  256.5 3.7 copy-start.22
  256.5 3.7 slice-start.4
  256.5 3.7 slice-start.6
  260.2 4.6 copy-start.3
  260.2 5.9 copy-start.20
  264.7 1.4 copy-start.40
  270.4 396.7 %all-reduce.16.cloned.1.call-start = ((), (), s32[]{:S(2)}) async-start(), calls=%async_computation.7 | async-start | bytes 15728640 | tf_op jit(solution)/shard_map/psum | solution.py:186
  270.5 6.9 copy-start.41
  376.1 2.4 copy-start.2
  380.0 6.4 copy-start.6
  380.0 6.4 copy-start.11
  380.0 12.1 %slice-start = ((s8[9437184]{0:T(1024)(128)(4,1)}), s8[4194304]{0:T(1024)(128)(4,1)S(1)}, s32[]{:S(2)}) async-start(s8[9437184]{0:T(1024)(128)(4,1)} %bitcast.159), calls=%async_computation.8 | async-start | bytes 8388608
  380.0 12.1 %slice-start.1 = ((s8[9437184]{0:T(1024)(128)(4,1)}), s8[4194304]{0:T(1024)(128)(4,1)S(1)}, s32[]{:S(2)}) async-start(s8[9437184]{0:T(1024)(128)(4,1)} %bitcast.159), calls=%async_computation.9 | async-start | bytes 8388608
  386.4 5.7 slice-start.2
  392.1 2.3 copy-start.18
  394.5 1.6 copy-start.7
  409.5 352.9 %all-reduce.14.cloned.1.call-start = ((), (), s32[]{:S(2)}) async-start(), calls=%async_computation.3 | async-start | bytes 9437184 | tf_op jit(solution)/shard_map/psum | solution.py:160
  415.2 251.9 %copy-start.12 = (f32[2,96,3,192]{3,1,2,0:T(8,128)S(1)}, f32[2,96,3,192]{3,1,2,0:T(8,128)}, u32[]{:S(2)}) copy-start(f32[2,96,3,192]{3,1,2,0:T(8,128)} %param.35) | copy-start | bytes 1327108
  415.2 253.9 %copy-start.13 = (f32[2,96,768]{2,1,0:T(8,128)S(1)}, f32[2,96,768]{2,1,0:T(8,128)}, u32[]{:S(2)}) copy-start(f32[2,96,768]{2,1,0:T(8,128)} %param.37) | copy-start | bytes 1769476
  415.2 255.9 %copy-start.24 = (f32[2,3072]{1,0:T(2,128)S(1)}, f32[2,3072]{1,0:T(2,128)}, u32[]{:S(2)}) copy-start(f32[2,3072]{1,0:T(2,128)} %param.41) | copy-start | bytes 73732
  415.2 258.4 %copy-start.23 = (f32[2,6,768]{2,0,1:T(2,128)S(1)}, f32[2,6,768]{2,0,1:T(2,128)}, u32[]{:S(2)}) copy-start(f32[2,6,768]{2,0,1:T(2,128)} %param.40) | copy-start | bytes 110596
  415.3 258.4 %copy-start.28 = (f32[768]{0:T(1024)S(1)}, f32[768]{0:T(1024)}, u32[]{:S(2)}) copy-start(f32[768]{0:T(1024)} %get-tuple-element.66) | copy-start | bytes 9220
  415.3 258.4 %copy-start.29 = (f32[768]{0:T(1024)S(1)}, f32[768]{0:T(1024)}, u32[]{:S(2)}) copy-start(f32[768]{0:T(1024)} %get-tuple-element.69) | copy-start | bytes 9220
  415.3 258.4 %copy-start.37 = (f32[768]{0:T(1024)S(1)}, f32[768]{0:T(1024)}, u32[]{:S(2)}) copy-start(f32[768]{0:T(1024)} %get-tuple-element.140) | copy-start | bytes 9220
  415.3 258.7 %copy-start.30 = (f32[768]{0:T(1024)S(1)}, f32[768]{0:T(1024)}, u32[]{:S(2)}) copy-start(f32[768]{0:T(1024)} %get-tuple-element.64) | copy-start | bytes 9220
  415.3 258.7 %copy-start.32 = (f32[768]{0:T(1024)S(1)}, f32[768]{0:T(1024)}, u32[]{:S(2)}) copy-start(f32[768]{0:T(1024)} %get-tuple-element.68) | copy-start | bytes 9220
  415.3 258.8 %copy-start.31 = (f32[768]{0:T(1024)S(1)}, f32[768]{0:T(1024)}, u32[]{:S(2)}) copy-start(f32[768]{0:T(1024)} %get-tuple-element.98) | copy-start | bytes 9220
  415.3 258.8 %copy-start.34 = (f32[3,64]{1,0:T(4,128)S(1)}, f32[3,64]{1,0:T(4,128)}, u32[]{:S(2)}) copy-start(f32[3,64]{1,0:T(4,128)} %get-tuple-element.138) | copy-start | bytes 2308
  415.3 258.9 %copy-start.35 = (f32[3,64]{1,0:T(4,128)S(1)}, f32[3,64]{1,0:T(4,128)}, u32[]{:S(2)}) copy-start(f32[3,64]{1,0:T(4,128)} %get-tuple-element.136) | copy-start | bytes 2308
  415.3 437.3 %all-gather.4.cloned.1.call-start = ((), (), s32[]{:S(2)}) async-start(), calls=%async_computation.4 | async-start | bytes 2654208 | tf_op jit(solution)/shard_map/all_gather | solution.py:211
  669.0 205.7 %all-gather.6.cloned.1.call-start = ((), (), s32[]{:S(2)}) async-start(), calls=%async_computation.5 | async-start | bytes 2654208 | tf_op jit(solution)/shard_map/all_gather | solution.py:213
  671.1 257.0 %all-gather.8.cloned.1.call-start = ((), (), s32[]{:S(2)}) async-start(), calls=%async_computation.6 | async-start | bytes 2654208 | tf_op jit(solution)/shard_map/all_gather | solution.py:214
  674.6 135.7 %copy-start.16 = (f32[6,768]{1,0:T(8,128)S(1)}, f32[6,768]{1,0:T(8,128)}, u32[]{:S(2)}) copy-start(f32[6,768]{1,0:T(8,128)} %param.33) | copy-start | bytes 55300
  674.6 137.0 %copy-start.26 = (f32[2,768]{1,0:T(2,128)S(1)}, f32[2,768]{1,0:T(2,128)}, u32[]{:S(2)}) copy-start(f32[2,768]{1,0:T(2,128)} %param.32) | copy-start | bytes 18436
  674.6 137.0 %copy-start.33 = (f32[2,2,768]{2,1,0:T(2,128)S(1)}, f32[2,2,768]{2,1,0:T(2,128)}, u32[]{:S(2)}) copy-start(f32[2,2,768]{2,1,0:T(2,128)} %param.39) | copy-start | bytes 36868
  674.6 138.2 %copy-start.27 = (f32[3072]{0:T(1024)S(1)}, f32[3072]{0:T(1024)}, u32[]{:S(2)}) copy-start(f32[3072]{0:T(1024)} %param.34) | copy-start | bytes 36868
  674.6 139.5 %copy-start.14 = (f32[2,96,192]{2,1,0:T(8,128)S(1)}, f32[2,96,192]{2,1,0:T(8,128)}, u32[]{:S(2)}) copy-start(f32[2,96,192]{2,1,0:T(8,128)} %param.36) | copy-start | bytes 442372
  928.1 3.4 copy-start.9
Sparse Core Ops, SparseCore 0:
  28.8 96.7 all-reduce.7
  153.0 94.1 all-reduce.9
  270.5 94.1 all-reduce.11
  409.6 257.4 all-reduce.15
  669.3 93.0 all-reduce.13
  765.0 52.6 all-gather.3
  820.4 54.2 all-gather.5
  877.5 50.5 all-gather.7
where the time goes:
time: 948 us; the launch traced here: 940 us
  waiting for transfers between devices  679 us (72%)
  matrix products  80.9 us (9%)
  blocking collectives  74.5 us (8%)
  other arithmetic  52.6 us (6%)
  local copies, waits for them, and re-layouts  34.9 us (4%)
  between operations  17.7 us (2%)
    psum x1, waiting for transfers between devices, on_device(): summed = lax.psum((grad_qkv, grad_out_proj, grad_in, grad_back), 'dp')  248 us
    psum x1, waiting for transfers between devices, on_device(): attn_sum = lax.psum(attn_part, 'tensor')  95.8 us
    psum x1, waiting for transfers between devices, on_device(): down_sum = lax.psum(down_part, 'tensor')  93.7 us
    psum x1, waiting for transfers between devices, on_device(): input_grad = lax.psum(d_entry_part, 'tensor') + d_res_one  87.7 us
    psum x1, waiting for transfers between devices, on_device(): d_normed = lax.psum(d_normed_part, 'tensor') + d_res_two  81 us
    all_gather x1, waiting for transfers between devices, on_device(): lax.all_gather(change_rows[3], 'dp', axis=0, tiled=True)  53.4 us
    psum x1, blocking collectives, on_device(): lax.psum((grad_gains, grad_biases, grad_bias_in), ('dp', 'tensor'))  41.3 us
    all_gather x1, blocking collectives, on_device(): lax.all_gather(change_rows[1], 'dp', axis=0, tiled=True)  33.2 us
  transfers between devices with their start and end apart: 8, of which 7 were waited for; matrix products, arithmetic and copies ran while one was open for 5% of the time, Pallas kernels for 0%

commit v1 on v0

--- a/solution.py
+++ b/solution.py
@@ -3,6 +3,7 @@
 import jax.numpy as jnp
 from jax import lax
 from jax.sharding import PartitionSpec as P
+from jax.lax import axis_size, ppermute
 
 HD = 64
 NORM_EPS = 1e-12
@@ -99,7 +100,10 @@
         .astype(jnp.bfloat16)
     )
     attn_part = jnp.einsum("tc,dc->td", context_low, out_low, preferred_element_type=jnp.float32)
-    attn_sum = lax.psum(attn_part, "tensor")
+    workers = axis_size("tensor")
+    attn_sum = attn_part
+    for at in [[(u, u ^ num) for u in range(workers)] for num in (1, 2, 4, 8, 16) if num < workers]:
+        attn_sum = attn_sum + ppermute(attn_sum, "tensor", at)
     residual_one = tokens_in.astype(jnp.float32) + attn_sum + biases[2]
     normed = layer_norm(residual_one, gains[0], biases[3])
     normed_low = normed.astype(jnp.bfloat16)

time: 948 us -> 970 us (1.023)
  local copies, waits for them, and re-layouts: 34.9 us -> 53.4 us
    ppermute x0 -> x2, waiting for transfers between devices: none -> 106 us  [on_device(): attn_sum = attn_sum + ppermute(attn_sum, 'tensor', at)]
    psum x1 -> x0, waiting for transfers between devices: 95.8 us -> none  [on_device(): attn_sum = lax.psum(attn_part, 'tensor')]
    unnamed x106 -> x144, local copies, waits for them, and re-layouts: 18.4 us -> 33.6 us
  transfers between devices with their start and end apart: 8 -> 9, of which waited for: 7 -> 8; matrix products, arithmetic and copies ran while one was open for 5% -> 7% of each run, Pallas kernels for 0% -> 0%
where the time goes in v1:
time: 970 us; the launch traced here: 960 us
  waiting for transfers between devices  672 us (69%)
  matrix products  78.7 us (8%)
  blocking collectives  74.9 us (8%)
  other arithmetic  59.4 us (6%)
  local copies, waits for them, and re-layouts  53.4 us (6%)
  between operations  17.9 us (2%)
    psum x1, waiting for transfers between devices, on_device(): summed = lax.psum((grad_qkv, grad_out_proj, grad_in, grad_back), 'dp')  248 us
    ppermute x2, waiting for transfers between devices, on_device(): attn_sum = attn_sum + ppermute(attn_sum, 'tensor', at)  106 us
    psum x1, waiting for transfers between devices, on_device(): down_sum = lax.psum(down_part, 'tensor')  89.8 us
    psum x1, waiting for transfers between devices, on_device(): d_normed = lax.psum(d_normed_part, 'tensor') + d_res_two  81.5 us
    psum x1, waiting for transfers between devices, on_device(): input_grad = lax.psum(d_entry_part, 'tensor') + d_res_one  80.6 us
    all_gather x1, waiting for transfers between devices, on_device(): lax.all_gather(change_rows[3], 'dp', axis=0, tiled=True)  53.3 us
    psum x1, blocking collectives, on_device(): lax.psum((grad_gains, grad_biases, grad_bias_in), ('dp', 'tensor'))  41.6 us
    unnamed x144, local copies, waits for them, and re-layouts  33.6 us
  transfers between devices with their start and end apart: 9, of which 8 were waited for; matrix products, arithmetic and copies ran while one was open for 7% of the time, Pallas kernels for 0%

profile of v1, /device:TPU:0, one launch (start us, length us, event | category | flops | bytes accessed | tf_op | source)
XLA Modules:
  0.0 959.6 jit_solution(16915727056688476704)
XLA Ops:
  7.2 3.8 fusion.10
  11.1 1.2 fusion.78
  13.2 1.2 convert_element_type.98
  14.4 0.9 squeeze.4
  15.3 1.9 squeeze.5
  17.2 3.5 add_reduce_fusion
  20.8 1.8 exponential_reduce_fusion
  22.9 1.5 copy-done
  24.5 1.7 fusion.12
  28.3 7.5 collective-permute-done
  35.8 3.2 add.278
  39.0 2.9 collective-permute-start.1
  41.8 2.8 copy.93
  46.1 98.2 %collective-permute-done.1 = f32[1536,768]{0,1:T(8,128)} collective-permute-done((f32[1536,768]{0,1:T(8,128)}, f32[1536,768]{0,1:T(8,128)}, u32[]{:S(2)}, u32[]{:S(2)}) %collective-permute-start.1) | collective-permute-done | bytes 4718624 | tf_op jit(solution)/shard_map/ppermute | solution.py:106
  144.3 4.6 fusion.77
  150.1 2.2 copy-done.32
  152.3 14.8 %multiply_convert_fusion.1 = (bf16[1536,768]{1,0:T(8,128)(2,1)S(1)}, f32[1536,768]{1,0:T(8,128)}, f32[1536,768]{1,0:T(8,128)}) fusion(f32[768]{0:T(1024)S(1)} %dynamic_slice.35, f32[768,768]{1,0:T(8,128)S(1)} %copy-done.32, f32[1536,768]{0,1:T(8,128)S(1)} %get-tuple-element.96, f32[768]{0:T(1024)S(1)} %copy-done.42, f32[768]{0:T(1024)S(1)} %get-tuple-element.75, ...), kind=kOutput, calls=%fused_computation.21 | convolution fusion | flops 1896284160 | bytes 18895872 | tf_op jit(solution)/shard_map/dot_general | solution.py:110
  167.1 1.4 copy-done.56
  168.5 4.2 fusion.26
  174.1 3.2 copy.100
  177.3 1.3 select_convert_fusion
  178.6 89.8 %all-reduce.7.cloned.1.call-done = f32[1536,768]{0,1:T(8,128)} async-done(((f32[1536,768]{0,1:T(8,128)}), f32[1536,768]{0,1:T(8,128)}) %all-reduce.7.cloned.1.call-update) | async-done | bytes 4718608 | tf_op jit(solution)/shard_map/psum | solution.py:113
  268.4 4.5 fusion.75
  273.7 2.9 multiply_reduce_fusion.1
  276.6 3.7 fusion.74
  280.4 4.7 fusion.83
  285.0 1.4 copy-done.57
  286.5 4.2 fusion.17
  290.8 6.7 fusion.19
  297.5 6.0 fusion.15
  303.5 81.5 %all-reduce.9.cloned.1.call-done = f32[1536,768]{0,1:T(8,128)} async-done(((f32[1536,768]{0,1:T(8,128)}), f32[1536,768]{0,1:T(8,128)}) %all-reduce.9.cloned.1.call-update) | async-done | bytes 4718608 | tf_op jit(solution)/shard_map/psum | solution.py:129
  385.0 7.4 multiply_reduce_fusion.2
  392.4 3.6 fusion.73
  396.0 2.3 fusion.21
  399.6 6.4 fusion.82
  406.0 5.7 multiply_reduce_fusion
  411.7 2.4 multiply_convert_fusion
  414.1 1.6 convolution_bitcast_fusion.2
  415.7 1.6 fusion.81
  419.2 1.0 mul.594
  421.8 4.4 fusion.86
  426.2 2.9 copy.113
  429.2 5.7 convolution_bitcast_fusion
  437.4 1.2 constant_dynamic-slice_fusion.1
  438.8 248.0 %all-reduce.13.cloned.1.call-done = (f32[768,3,192]{2,0,1:T(8,128)}, f32[768,192]{1,0:T(8,128)}, f32[768,768]{1,0:T(8,128)}, f32[768,768]{1,0:T(8,128)}) async-done(((f32[768,3,192]{2,0,1:T(8,128)}, f32[768,192]{1,0:T(8,128)}, f32[768,768]{1,0:T(8,128)}, f32[768,768]{1,0:T(8,128)}), (f32[768,3,192]{2,0,1:T(8,128)}, f32[768,192]{1,0:T(8,128)}, f32[768,768]{1,0:T(8,128)}, ...) | async-done | bytes 7077904 | tf_op jit(solution)/shard_map/psum | solution.py:190
  686.8 2.2 fusion.50
  689.0 2.3 fusion.48
  691.4 1.5 slice_multiply_fusion.1
  692.8 2.6 fusion.49
  696.2 1.0 copy.132
  697.2 0.9 fusion.79
  698.2 2.4 copy.118
  701.4 80.6 %all-reduce.11.cloned.1.call-done = f32[1536,768]{0,1:T(8,128)} async-done(((f32[1536,768]{0,1:T(8,128)}), f32[1536,768]{0,1:T(8,128)}) %all-reduce.11.cloned.1.call-update) | async-done | bytes 4718608 | tf_op jit(solution)/shard_map/psum | solution.py:164
  782.1 6.5 add_reduce_fusion.1
  788.6 41.6 %all-reduce = (f32[2,768]{1,0:T(2,128)S(1)}, f32[6,768]{1,0:T(8,128)S(1)}, f32[3072]{0:T(1024)S(1)}) all-reduce(f32[2,768]{1,0:T(2,128)S(1)} %maximum_multiply_fusion, f32[6,768]{1,0:T(8,128)S(1)} %stack.89, f32[3072]{0:T(1024)S(1)} %dynamic_update_slice.13), channel_id=1, replica_groups=mesh['dp'=8,'tensor'=4] {'dp','tensor'}, use_global_device_ids=true, to_apply=%region_20.21 | all-reduce | flops 9216 | bytes 73728 | tf_op jit(solution)/shard_map/psum | solution.py:185
  831.6 6.1 copy.119
  840.2 1.0 fusion.58
  841.2 33.3 %all_gather.13 = f32[768,192]{1,0:T(8,128)S(1)} all-gather(f32[96,192]{1,0:T(8,128)S(1)} %get-tuple-element.114), channel_id=1, replica_groups=mesh['dp'=8,'tensor'=4] {'dp'}, dimensions={0}, use_global_device_ids=true | all-gather | bytes 663552 | tf_op jit(solution)/shard_map/all_gather | solution.py:216
  874.5 1.1 copy.121
  878.9 2.9 copy.120
  881.8 12.5 %all-gather.6.cloned.1.call-done = f32[768,768]{1,0:T(8,128)} async-done(((f32[96,768]{1,0:T(8,128)}), f32[768,768]{1,0:T(8,128)}) %all-gather.6.cloned.1.call-update) | async-done | bytes 2359312 | tf_op jit(solution)/shard_map/all_gather | solution.py:217
  894.3 53.3 %all-gather.8.cloned.1.call-done = f32[768,768]{1,0:T(8,128)} async-done(((f32[96,768]{1,0:T(8,128)}), f32[768,768]{1,0:T(8,128)}) %all-gather.8.cloned.1.call-update) | async-done | bytes 2359312 | tf_op jit(solution)/shard_map/all_gather | solution.py:218
  947.6 3.4 copy.200
  951.0 1.4 copy.201
  (213 shorter events, 21.9 us)
Async XLA Ops:
  7.2 261.2 %all-reduce.7.cloned.1.call-start = ((), (), s32[]{:S(2)}) async-start(), calls=%async_computation | async-start | bytes 9437184 | tf_op jit(solution)/shard_map/psum | solution.py:113
  13.2 7.5 copy-start.23
  17.2 3.5 copy-start.4
  20.8 3.7 copy-start
  22.6 3.6 copy-start.16
  24.4 2.5 copy-start.10
  27.7 8.1 collective-permute-start
  39.0 6.5 copy-start.37
  39.0 105.3 %collective-permute-start.1 = (f32[1536,768]{0,1:T(8,128)}, f32[1536,768]{0,1:T(8,128)}, u32[]{:S(2)}, u32[]{:S(2)}) collective-permute-start(f32[1536,768]{0,1:T(8,128)} %add.278), channel_id=1, source_target_pairs={{0,2},{1,3},{2,0},{3,1},{4,6},{5,7},{6,4},{7,5},{8,10},{9,11},{10,... | collective-permute-start | bytes 14155784 | tf_op jit(solution)/shard_map/ppermute | solution.py:106
  45.5 104.6 %copy-start.52 = (f32[768]{0:T(1024)}, f32[768]{0:T(1024)S(1)}, u32[]{:S(2)}) copy-start(f32[768]{0:T(1024)S(1)} %dynamic_slice.35) | copy-start | bytes 9220
  46.1 104.0 %copy-start.28 = (f32[768]{0:T(1024)}, f32[768]{0:T(1024)S(1)}, u32[]{:S(2)}) copy-start(f32[768]{0:T(1024)S(1)} %get-tuple-element.75) | copy-start | bytes 9220
  148.9 18.2 %copy-start.1 = (f32[1536,768]{0,1:T(8,128)}, f32[1536,768]{0,1:T(8,128)S(1)}, u32[]{:S(2)}) copy-start(f32[1536,768]{0,1:T(8,128)S(1)} %get-tuple-element.96) | copy-start | bytes 14155780
  148.9 3.4 copy-start.32
  148.9 3.4 copy-start.42
  150.0 17.0 %copy-start.19 = (f32[1536]{0:T(1024)}, f32[1536]{0:T(1024)S(1)}, u32[]{:S(2)}) copy-start(f32[1536]{0:T(1024)S(1)} %fusion.63) | copy-start | bytes 18436
  152.3 16.2 %copy-start.34 = (f32[768,768]{1,0:T(8,128)S(1)}, f32[768,768]{1,0:T(8,128)}, u32[]{:S(2)}) copy-start(f32[768,768]{1,0:T(8,128)} %param.31) | copy-start | bytes 7077892
  172.8 212.3 %all-reduce.9.cloned.1.call-start = ((), (), s32[]{:S(2)}) async-start(), calls=%async_computation.1 | async-start | bytes 9437184 | tf_op jit(solution)/shard_map/psum | solution.py:129
  273.5 3.1 copy-start.44
  273.7 6.6 slice-start.3
  273.7 6.7 slice-start.5
  276.6 3.7 copy-start.35
  276.6 3.7 copy-start.53
  276.6 3.7 slice-start.4
  276.6 3.7 slice-start.6
  280.3 4.8 copy-start.3
  280.4 6.1 copy-start.33
  290.7 6.8 copy-start.20
  290.7 6.8 copy-start.29
  290.7 6.8 copy-start.43
  290.7 396.0 %all-reduce.13.cloned.1.call-start = ((), (), s32[]{:S(2)}) async-start(), calls=%async_computation.6 | async-start | bytes 15728640 | tf_op jit(solution)/shard_map/psum | solution.py:190
  290.8 6.7 copy-start.58
  303.5 88.9 %copy-start.26 = (f32[1536]{0:T(1024)S(1)}, f32[1536]{0:T(1024)}, u32[]{:S(2)}) copy-start(f32[1536]{0:T(1024)} %copy-done.25) | copy-start | bytes 18436
  396.0 2.4 copy-start.2
  399.5 6.4 copy-start.8
  399.6 12.1 %slice-start = ((s8[9437184]{0:T(1024)(128)(4,1)}), s8[4194304]{0:T(1024)(128)(4,1)S(1)}, s32[]{:S(2)}) async-start(s8[9437184]{0:T(1024)(128)(4,1)} %bitcast.159), calls=%async_computation.7 | async-start | bytes 8388608
  399.6 12.1 %slice-start.1 = ((s8[9437184]{0:T(1024)(128)(4,1)}), s8[4194304]{0:T(1024)(128)(4,1)S(1)}, s32[]{:S(2)}) async-start(s8[9437184]{0:T(1024)(128)(4,1)} %bitcast.159), calls=%async_computation.8 | async-start | bytes 8388608
  406.0 5.7 slice-start.2
  411.7 2.4 copy-start.5
  411.7 2.4 copy-start.24
  429.2 352.9 %all-reduce.11.cloned.1.call-start = ((), (), s32[]{:S(2)}) async-start(), calls=%async_computation.2 | async-start | bytes 9437184 | tf_op jit(solution)/shard_map/psum | solution.py:164
  435.0 263.1 %copy-start.40 = (f32[768]{0:T(1024)S(1)}, f32[768]{0:T(1024)}, u32[]{:S(2)}) copy-start(f32[768]{0:T(1024)} %get-tuple-element.66) | copy-start | bytes 9220
  435.0 263.2 %copy-start.41 = (f32[768]{0:T(1024)S(1)}, f32[768]{0:T(1024)}, u32[]{:S(2)}) copy-start(f32[768]{0:T(1024)} %get-tuple-element.69) | copy-start | bytes 9220
  435.0 263.2 %copy-start.6 = (bf16[1536,768]{0,1:T(8,128)(2,1)S(1)}, bf16[1536,768]{0,1:T(8,128)(2,1)}, u32[]{:S(2)}) copy-start(bf16[1536,768]{0,1:T(8,128)(2,1)} %get-tuple-element.97) | copy-start | bytes 7077892
  435.0 443.9 %all-gather.4.cloned.1.call-start = ((), (), s32[]{:S(2)}) async-start(), calls=%async_computation.3 | async-start | bytes 2654208 | tf_op jit(solution)/shard_map/all_gather | solution.py:215
  689.0 205.3 %all-gather.6.cloned.1.call-start = ((), (), s32[]{:S(2)}) async-start(), calls=%async_computation.4 | async-start | bytes 2654208 | tf_op jit(solution)/shard_map/all_gather | solution.py:217
  691.3 256.3 %all-gather.8.cloned.1.call-start = ((), (), s32[]{:S(2)}) async-start(), calls=%async_computation.5 | async-start | bytes 2654208 | tf_op jit(solution)/shard_map/all_gather | solution.py:218
  696.2 4.4 copy-start.51
  696.2 4.7 copy-start.45
  696.2 4.7 copy-start.47
  696.2 4.7 copy-start.46
  696.2 4.8 copy-start.49
  696.2 4.8 copy-start.50
  701.4 128.8 %copy-start.22 = (f32[6,768]{1,0:T(8,128)S(1)}, f32[6,768]{1,0:T(8,128)}, u32[]{:S(2)}) copy-start(f32[6,768]{1,0:T(8,128)} %param.33) | copy-start | bytes 55300
  831.5 6.2 copy-start.38
  831.5 6.2 copy-start.48
  831.5 7.4 copy-start.30
  831.5 7.4 copy-start.31
  831.5 7.4 copy-start.39
  831.5 8.7 copy-start.18
  831.6 44.7 %copy-start.12 = (f32[1,96,3,192]{3,1,2,0:T(8,128)S(1)}, f32[1,96,3,192]{3,1,2,0:T(8,128)}, u32[]{:S(2)}) copy-start(f32[1,96,3,192]{3,1,2,0:T(8,128)} %get-tuple-element.110) | copy-start | bytes 663556
  837.7 39.4 %copy-start.14 = (f32[1,96,768]{2,1,0:T(8,128)S(1)}, f32[1,96,768]{2,1,0:T(8,128)}, u32[]{:S(2)}) copy-start(f32[1,96,768]{2,1,0:T(8,128)} %get-tuple-element.103) | copy-start | bytes 884740
  837.7 39.4 %copy-start.15 = (f32[1,96,768]{2,1,0:T(8,128)S(1)}, f32[1,96,768]{2,1,0:T(8,128)}, u32[]{:S(2)}) copy-start(f32[1,96,768]{2,1,0:T(8,128)} %get-tuple-element.104) | copy-start | bytes 884740
  837.7 40.3 %copy-start.13 = (f32[1,96,768]{2,1,0:T(8,128)S(1)}, f32[1,96,768]{2,1,0:T(8,128)}, u32[]{:S(2)}) copy-start(f32[1,96,768]{2,1,0:T(8,128)} %get-tuple-element.107) | copy-start | bytes 884740
  947.6 3.4 copy-start.11
  (11 other events, 12.5 us)
Sparse Core Ops, SparseCore 0:
  172.9 95.4 all-reduce.6
  290.8 94.1 all-reduce.8
  429.3 257.4 all-reduce.12
  689.0 93.0 all-reduce.10
  784.7 52.6 all-gather.3
  840.0 54.2 all-gather.5
  896.5 51.0 all-gather.7
